TPU v7x, 256 devices: a whole 4x4x8 slice. The times are simulated.
256 devices in a mesh: side: 2 (over y_hi), slab: 128 (over x, y_lo, z, core).
Axes of the slice: x: 4, y: 4 (y_hi: 2, y_lo: 2; y = y_hi * 2 + y_lo), z: 8, core: 2. Of those that a mesh axis runs over, the one named last changes fastest.
Arguments:
- velocity: float32 [2, 4096, 4096], P('side', 'slab'), may hold values from -6 to 6
- kernel: bfloat16 [2, 9, 4096, 4096], P('side', None, 'slab'), may hold values from -4 to 4
- history: bfloat16 [2, 8, 2, 4096, 4096], P('side', None, None, 'slab'), may hold values from -24576 to 24576
- impedance: float32 [2], replicated, may hold values from 0.5 to 1.5
- prestress: float32 [4096, 4096], P('slab'), may hold values from 1 to 3
- strength: float32 [4096, 4096], P('slab'), may hold values from 0.5 to 2
- fault_state: float32 [4096, 4096], P('slab'), may hold values from -1 to 1
Outputs:
- new_velocity: float32 [2, 4096, 4096], P('side', 'slab')
- slip_rate: float32 [4096, 4096], P('slab')
- new_state: float32 [4096, 4096], P('slab')
All inputs are finite; a program needn't handle non-finite values.
Results may differ from a plain program's by a relative error of at most 0.00058.
Values sent between devices are 32-bit elements; how exact they have to be, the bound alone decides.
A program may use at most 128 MiB of HBM per device.

v0:
```python
import functools
import math

import jax
import jax.numpy as jnp
import ml_dtypes
import numpy as np
from jax import lax
from jax.experimental import pallas as pl
from jax.experimental.pallas import tpu as pltpu
from jax.sharding import PartitionSpec as P

NX = 4096
NZ = 4096
LAGS = 8
NEWTON = 4
STEPS = 2
SLABS = 128
ROWS = 32
LANES = 128
MESH = pl.DeviceIdType.MESH
F32 = jnp.float32
BF16 = jnp.bfloat16
VMEM_BYTES = 56 * 2**20


def high_low(table, axis):
    table = table.astype(np.float32)
    high = table.astype(ml_dtypes.bfloat16)
    low = (table - high.astype(np.float32)).astype(ml_dtypes.bfloat16)
    return np.concatenate([high, low, high], axis=axis)


def complex_matrix(count, sign):
    angle = 2.0 * math.pi / count * (np.outer(np.arange(count), np.arange(count)) % count)
    cos, sin = np.cos(angle), sign * np.sin(angle)
    return np.block([[cos, -sin], [sin, cos]])


def tables():
    forward, inverse = complex_matrix(128, -1.0), complex_matrix(128, 1.0)
    forward_32 = complex_matrix(32, -1.0).reshape(2, 32, 2, 32)
    inverse_32 = complex_matrix(32, 1.0).reshape(2, 32, 2, 32)
    eye = np.eye(8)
    z_first = np.einsum("ajn,xy->ajxny", forward_32[:, :, 0], eye).reshape(512, 256)
    x_second = np.einsum("akcgx,ij->akicgjx", forward_32.reshape(2, 32, 2, 4, 8), eye).reshape(512, 512)
    x_third = np.einsum("axck,ij->axickj", inverse_32, eye).reshape(512, 512)
    z_last = np.einsum("zcgj,xy->zxcgyj", inverse_32[0].reshape(32, 2, 4, 8), eye).reshape(256, 512) / (NX * NZ)
    phase = 2.0 * math.pi / 4096 * np.outer(np.arange(32), np.arange(128))
    twiddle = np.stack([np.cos(phase), np.sin(phase)]).astype(np.float32)
    return dict(
        z_first=high_low(z_first, 1),
        x_second=high_low(x_second, 1),
        x_third=high_low(x_third, 1),
        z_last=high_low(z_last, 1),
        forward_left=high_low(forward, 1),
        inverse_left=high_low(inverse, 1),
        forward_right=high_low(forward.T, 0),
        inverse_right=high_low(inverse.T, 0),
        twiddle=twiddle,
        twiddle_rows=np.repeat(twiddle, 8, axis=1),
    )


def split(value):
    high = value.astype(BF16)
    low = (value - high.astype(F32)).astype(BF16)
    return high, low


def left_product(table, value):
    high, low = split(value)
    stacked = jnp.concatenate([high, high, low], axis=0)
    return jnp.dot(table, stacked, preferred_element_type=F32)


def right_product(value, table):
    high, low = split(value)
    stacked = jnp.concatenate([high, high, low], axis=1)
    return jnp.dot(stacked, table, preferred_element_type=F32)


def left_product_transposed(table, value):
    high, low = split(value)
    stacked = jnp.concatenate([high, high, low], axis=1)
    return lax.dot_general(table, stacked, (((1,), (1,)), ((), ())), preferred_element_type=F32)


def turn(real, imag, cos, sin):
    return real * cos - imag * sin, real * sin + imag * cos


def put_group(ref, group, value):
    for part in range(2):
        for half in range(2):
            piece = value[part * 128 : part * 128 + 128, half * 128 : half * 128 + 128]
            ref[pl.ds(part * 8 + group * 2 + half, SLABS, stride=16), :] = piece


def get_group(ref, group):
    return jnp.concatenate(
        [
            jnp.concatenate(
                [ref[pl.ds(part * 8 + group * 2 + half, SLABS, stride=16), :] for half in range(2)], axis=1
            )
            for part in range(2)
        ],
        axis=0,
    )


def z_forward(field, send, t):
    cos, sin = t["twiddle_rows"][0], t["twiddle_rows"][1]
    for pair in range(2):
        columns = [
            jnp.concatenate(
                [field[group * 8 : group * 8 + 8, n * 128 : n * 128 + 128] for n in range(32)], axis=0
            )
            for group in (2 * pair, 2 * pair + 1)
        ]
        first = left_product(t["z_first"][...], jnp.concatenate(columns, axis=1))
        for q in range(2):
            piece = first[:, q * 128 : q * 128 + 128]
            real, imag = turn(piece[:256], piece[256:], cos, -sin)
            turned = jnp.concatenate([real, imag], axis=1)
            put_group(send, 2 * pair + q, left_product_transposed(t["forward_left"][...], turned))


def gather_stage(received, table, twiddle, sign, middle):
    for group in range(4):
        rows = get_group(received, group).T
        first = right_product(rows, table[...])
        cos = twiddle[0, group * 8 : group * 8 + 8, :][None]
        sin = sign * twiddle[1, group * 8 : group * 8 + 8, :][None]
        real, imag = turn(first[:, :128].reshape(32, 8, 128), first[:, 128:].reshape(32, 8, 128), cos, sin)
        middle[0, group] = real.reshape(256, 128)
        middle[1, group] = imag.reshape(256, 128)


def middle_columns(middle, pair):
    return jnp.concatenate(
        [
            jnp.concatenate(
                [middle[c, g, q * 64 : q * 64 + 64, :] for c in range(2) for g in range(4)], axis=0
            )
            for q in (2 * pair, 2 * pair + 1)
        ],
        axis=1,
    )


def spectrum_phase(step, received, kernel, history, spec, send, t, middle, wide):
    gather_stage(received, t["forward_right"], t["twiddle"], -1.0, middle)
    cos, sin = t["twiddle_rows"][0], t["twiddle_rows"][1]
    for pair in range(2):
        wide[...] = left_product(t["x_second"][...], middle_columns(middle, pair))

        def convolve(k, carry):
            lanes = pl.ds(pl.multiple_of(k * 128, 128), 128)
            rows = slice(pair * 16, pair * 16 + 16)
            weights = [kernel[lag, rows, lanes].astype(F32) for lag in range(LAGS + 1)]
            for part in range(2):
                place = pl.ds(pl.multiple_of(part * 256 + k * 8, 8), 8)
                fresh = wide[place, :]
                rounded = jnp.concatenate([fresh[:, :128], fresh[:, 128:]], axis=0).astype(BF16)
                total = weights[0] * rounded.astype(F32)
                for lag in range(LAGS):
                    if lag < step:
                        past = spec[part, rows, lanes]
                    else:
                        past = history[lag - step, part, rows, lanes]
                    total = total + weights[lag + 1] * past.astype(F32)
                if step == 0:
                    spec[part, rows, lanes] = rounded
                wide[place, :] = jnp.concatenate([total[:8], total[8:]], axis=1)
            return carry

        lax.fori_loop(0, 32, convolve, 0)
        third = left_product(t["x_third"][...], wide[...])
        for q in range(2):
            piece = third[:, q * 128 : q * 128 + 128]
            real, imag = turn(piece[:256], piece[256:], cos, sin)
            turned = jnp.concatenate([real, imag], axis=1)
            put_group(send, 2 * pair + q, left_product_transposed(t["inverse_left"][...], turned))


def z_inverse(received, force, t, middle):
    gather_stage(received, t["inverse_right"], t["twiddle"], 1.0, middle)
    for pair in range(2):
        last = left_product(t["z_last"][...], middle_columns(middle, pair))
        for q in range(2):
            group = 2 * pair + q
            for n in range(32):
                force[group * 8 : group * 8 + 8, n * 128 : n * 128 + 128] = last[
                    n * 8 : n * 8 + 8, q * 128 : q * 128 + 128
                ]


def friction(is_first, impedance, force, other, prestress, strength, state, speed, rate_out, state_out):
    eta_first, eta_second = impedance[0], impedance[1]
    eta_total = eta_first + eta_second
    weight_first = eta_second / eta_total
    weight_second = eta_first / eta_total
    eta_joint = eta_first * eta_second / eta_total
    own_weight = jnp.where(is_first, weight_first, weight_second)
    other_weight = jnp.where(is_first, weight_second, weight_first)
    own_scale = jnp.where(is_first, 1.0 / eta_first, -1.0 / eta_second)

    def solve(index, carry):
        row = pl.multiple_of(lax.rem(index, 4) * 8, 8)
        lane = pl.multiple_of(lax.div(index, 4) * 512, 512)
        at = (pl.ds(row, 8), pl.ds(lane, 512))
        own = force[at]
        stress_now = prestress[at]
        normal = strength[at]
        psi = state[at]
        locked = stress_now + (own_weight * own + other_weight * other[at])
        rate = locked / (eta_joint + normal)
        factor = 0.5 * jnp.exp(psi)
        normal_factor = normal * factor
        for _ in range(NEWTON):
            scaled = factor * rate
            magnitude = jnp.abs(scaled)
            square = magnitude * magnitude
            root = jnp.sqrt(1.0 + square)
            arc = jnp.log1p(magnitude + square / (1.0 + root))
            arc = jnp.where(scaled < 0.0, -arc, arc)
            misfit = normal * arc + eta_joint * rate - locked
            slope = normal_factor / root + eta_joint
            rate = rate - 0.5 * misfit / slope
        stress = locked - eta_joint * rate
        speed[at] = (stress_now + own - stress) * own_scale
        rate_out[at] = rate
        state_out[at] = psi + 0.25 * (jnp.exp(-psi) - jnp.abs(rate))
        return carry

    lax.fori_loop(0, 32, solve, 0)


def exchange(s_ref, r_ref, send_sem, recv_sem, own_sem):
    me = lax.axis_index("slab")
    side = lax.axis_index("side")
    barrier = pltpu.get_barrier_semaphore()

    def greet(i, carry):
        there = lax.rem(me + i, SLABS)
        pl.semaphore_signal(barrier, inc=1, device_id=(side, there), device_id_type=MESH)
        return carry

    lax.fori_loop(1, SLABS, greet, 0)
    own = pltpu.make_async_copy(s_ref.at[me], r_ref.at[me], own_sem)
    own.start()
    pl.semaphore_wait(barrier, SLABS - 1)

    def start(i, carry):
        there = lax.rem(me + i, SLABS)
        pltpu.make_async_remote_copy(
            src_ref=s_ref.at[there],
            dst_ref=r_ref.at[me],
            send_sem=send_sem,
            recv_sem=recv_sem,
            device_id=(side, there),
            device_id_type=MESH,
        ).start()
        return carry

    lax.fori_loop(1, SLABS, start, 0)
    own.wait()
    bulk = r_ref.at[pl.ds(0, SLABS - 1)]
    pltpu.make_async_copy(bulk, bulk, recv_sem).wait()
    pltpu.make_async_copy(bulk, bulk, send_sem).wait()


def whole(space=pltpu.VMEM):
    return pl.BlockSpec(memory_space=space)


def all_to_all(value, number):
    shaped = value.reshape(SLABS, 16, LANES)
    result = pl.pallas_call(
        exchange,
        out_shape=jax.ShapeDtypeStruct(shaped.shape, F32),
        in_specs=[whole()],
        out_specs=whole(),
        scratch_shapes=[pltpu.SemaphoreType.DMA] * 3,
        compiler_params=pltpu.CompilerParams(
            collective_id=number, has_side_effects=True, vmem_limit_bytes=VMEM_BYTES
        ),
        name="all_to_all",
    )(shaped)
    return result.reshape(SLABS * 16, LANES)


def call(body, outs, scratch, *args, smem=()):
    return pl.pallas_call(
        body,
        out_shape=outs,
        in_specs=[whole(pltpu.SMEM if i in smem else pltpu.VMEM) for i in range(len(args))],
        out_specs=jax.tree.map(lambda _: whole(), outs),
        scratch_shapes=scratch,
        compiler_params=pltpu.CompilerParams(vmem_limit_bytes=VMEM_BYTES),
        name=body.__name__,
    )(*args)


MESSAGE = jax.ShapeDtypeStruct((SLABS * 16, LANES), F32)
FIELD = jax.ShapeDtypeStruct((ROWS, NZ), F32)
SPECTRUM = jax.ShapeDtypeStruct((2, ROWS, NX), BF16)
MIDDLE = pltpu.VMEM((2, 4, 256, LANES), F32)
WIDE = pltpu.VMEM((512, 256), F32)


def local(t, velocity, kernel, history, impedance, prestress, strength, fault_state):
    kernel, history = kernel[0], history[0]

    def first_kernel(field, z_first, forward_left, twiddle_rows, send):
        z_forward(field, send, dict(z_first=z_first, forward_left=forward_left, twiddle_rows=twiddle_rows))

    send = call(
        first_kernel, MESSAGE, [], velocity[0], t["z_first"], t["forward_left"], t["twiddle_rows"]
    )
    state = fault_state
    spec = None
    names = ("forward_right", "twiddle", "twiddle_rows", "x_second", "x_third", "inverse_left")
    for step in range(STEPS):
        received = all_to_all(send, 2 * step)
        if step == 0:

            def spectrum_first(received, kernel, history, a, b, c, d, e, f, send, spec, middle, wide):
                spectrum_phase(
                    0, received, kernel, history, spec, send, dict(zip(names, (a, b, c, d, e, f))), middle, wide
                )

            send, spec = call(
                spectrum_first,
                (MESSAGE, SPECTRUM),
                [MIDDLE, WIDE],
                received,
                kernel,
                history,
                *(t[n] for n in names),
            )
        else:

            def spectrum_second(received, kernel, history, spec, a, b, c, d, e, f, send, middle, wide):
                spectrum_phase(
                    1, received, kernel, history, spec, send, dict(zip(names, (a, b, c, d, e, f))), middle, wide
                )

            send = call(
                spectrum_second,
                MESSAGE,
                [MIDDLE, WIDE],
                received,
                kernel,
                history,
                spec,
                *(t[n] for n in names),
            )
        received = all_to_all(send, 2 * step + 1)

        def force_kernel(received, inverse_right, twiddle, z_last, force, middle):
            z_inverse(
                received, force, dict(inverse_right=inverse_right, twiddle=twiddle, z_last=z_last), middle
            )

        force = call(
            force_kernel, FIELD, [MIDDLE], received, t["inverse_right"], t["twiddle"], t["z_last"]
        )
        other = lax.ppermute(force, "side", [(0, 1), (1, 0)])

        def friction_kernel(
            impedance, force, other, prestress, strength, state, z_first, forward_left, twiddle_rows,
            speed, rate, state_out, send,
        ):
            friction(
                lax.axis_index("side") == 0, impedance, force, other, prestress, strength, state,
                speed, rate, state_out,
            )
            z_forward(speed, send, dict(z_first=z_first, forward_left=forward_left, twiddle_rows=twiddle_rows))

        def last_friction(impedance, force, other, prestress, strength, state, speed, rate, state_out):
            friction(
                lax.axis_index("side") == 0, impedance, force, other, prestress, strength, state,
                speed, rate, state_out,
            )

        fields = (impedance, force, other, prestress, strength, state)
        if step < STEPS - 1:
            speed, rate, state, send = call(
                friction_kernel, (FIELD, FIELD, FIELD, MESSAGE), [], *fields,
                t["z_first"], t["forward_left"], t["twiddle_rows"], smem=(0,),
            )
        else:
            speed, rate, state = call(last_friction, (FIELD, FIELD, FIELD), [], *fields, smem=(0,))
    return (speed[None], rate, state)


def solution(mesh):
    placed = (
        P("side", "slab", None),
        P("side", None, "slab", None),
        P("side", None, None, "slab", None),
        P(),
        P("slab", None),
        P("slab", None),
        P("slab", None),
    )
    constants = tables()

    def run(*args):
        return local({name: jnp.asarray(value) for name, value in constants.items()}, *args)

    return jax.shard_map(
        run,
        mesh=mesh,
        in_specs=placed,
        out_specs=(P("side", "slab", None), P("slab", None), P("slab", None)),
        check_vma=False,
    )
```

profile of v0, /device:TPU:1, one launch (start us, length us, event | category | flops | bytes accessed | tf_op | source)
XLA Modules:
  0.0 232.0 jit_solution(9303579182739770652)
XLA Ops:
  0.6 4.1 %first_kernel.1 = f32[2048,128]{1,0:T(8,128)} custom-call(f32[32,4096]{1,0:T(8,128)} %bitcast.24, bf16[512,768]{1,0:T(8,128)(2,1)} %constant.20.clone.z_first, bf16[256,768]{1,0:T(8,128)(2,1)} %constant.24.clone.forward_left, f32[2,256,128]{2,1,0:T(8,128)} %constant.29.clone.twiddle_rows.c), custom_call_target="tpu_custom_call" | custom-call | tf_op jit(solution)/shard_map/first_kernel/pallas_call | solution.py:295
  4.7 38.8 %all_to_all.4 = f32[128,16,128]{2,1,0:T(8,128)} custom-call(f32[128,16,128]{2,1,0:T(8,128)} %bitcast.19), custom_call_target="tpu_custom_call" | custom-call | tf_op jit(solution)/shard_map/all_to_all/pallas_call | solution.py:280
  43.5 13.1 %spectrum_first.1 = (f32[2048,128]{1,0:T(8,128)}, bf16[2,32,4096]{2,1,0:T(8,128)(2,1)}) custom-call(f32[2048,128]{1,0:T(8,128)} %bitcast.18, bf16[9,32,4096]{2,1,0:T(8,128)(2,1)} %bitcast.14, bf16[8,2,32,4096]{3,2,1,0:T(8,128)(2,1)} %bitcast.12, bf16[768,256]{1,0:T(8,128)(2,1)} %constant.26.clone.a, f32[2,32,128]{2,1,0:T(8,128)} %constant.28.clone.b.twiddle, ...), custom_call_target="tpu_custom_call" | custom-call | tf_op jit(solution)/shard_map/spectrum_first/pallas_call | solution.py:295
  56.6 34.3 %all_to_all.5 = f32[128,16,128]{2,1,0:T(8,128)} custom-call(f32[128,16,128]{2,1,0:T(8,128)} %bitcast.23), custom_call_target="tpu_custom_call" | custom-call | tf_op jit(solution)/shard_map/all_to_all/pallas_call | solution.py:280
  90.9 3.6 %force_kernel.2.force = f32[32,4096]{1,0:T(8,128)} custom-call(f32[2048,128]{1,0:T(8,128)} %bitcast.21, bf16[768,256]{1,0:T(8,128)(2,1)} %constant.27.clone.inverse_right, f32[2,32,128]{2,1,0:T(8,128)} %constant.28.clone.b.twiddle, bf16[256,1536]{1,0:T(8,128)(2,1)} %constant.23.clone.z_last), custom_call_target="tpu_custom_call" | custom-call | tf_op jit(solution)/shard_map/force_kernel/pallas_call | solution.py:295
  94.5 2.6 %collective-permute-start = (f32[32,4096]{1,0:T(8,128)}, f32[32,4096]{1,0:T(8,128)S(1)}, u32[]{:S(2)}, u32[]{:S(2)}) collective-permute-start(f32[32,4096]{1,0:T(8,128)} %force_kernel.2.force), channel_id=1, source_target_pairs={{0,128},{128,0},{1,129},{129,1},{2,130},{130,2},{3,131},{131,3},{4... | collective-permute-start | bytes 1572872 | tf_op jit(solution)/shard_map/ppermute | solution.py:370
  97.1 12.2 %collective-permute-done.other = f32[32,4096]{1,0:T(8,128)S(1)} collective-permute-done((f32[32,4096]{1,0:T(8,128)}, f32[32,4096]{1,0:T(8,128)S(1)}, u32[]{:S(2)}, u32[]{:S(2)}) %collective-permute-start) | collective-permute-done | bytes 524320 | tf_op jit(solution)/shard_map/ppermute | solution.py:370
  109.4 0.0 copy-start
  109.4 0.8 copy-done
  110.2 10.3 %friction_kernel.1 = (f32[32,4096]{1,0:T(8,128)}, f32[32,4096]{1,0:T(8,128)}, f32[32,4096]{1,0:T(8,128)}, f32[2048,128]{1,0:T(8,128)}) custom-call(f32[2]{0:T(128)} %impedance.3, f32[32,4096]{1,0:T(8,128)} %force_kernel.2.force, f32[32,4096]{1,0:T(8,128)} %copy-done, f32[32,4096]{1,0:T(8,128)} %prestress.3, f32[32,4096]{1,0:T(8,128)} %strength.3, ...), custom_call_target="tpu_custom_call" | custom-call | tf_op jit(solution)/shard_map/friction_kernel/pallas_call | solution.py:295
  120.5 35.8 %all_to_all.6 = f32[128,16,128]{2,1,0:T(8,128)} custom-call(f32[128,16,128]{2,1,0:T(8,128)} %bitcast.22), custom_call_target="tpu_custom_call" | custom-call | tf_op jit(solution)/shard_map/all_to_all/pallas_call | solution.py:280
  156.3 13.2 %spectrum_second.1 = f32[2048,128]{1,0:T(8,128)} custom-call(f32[2048,128]{1,0:T(8,128)} %bitcast.16, bf16[9,32,4096]{2,1,0:T(8,128)(2,1)} %bitcast.15, bf16[8,2,32,4096]{3,2,1,0:T(8,128)(2,1)} %bitcast.13, bf16[2,32,4096]{2,1,0:T(8,128)(2,1)} %get-tuple-element.12.spec, bf16[768,256]{1,0:T(8,128)(2,1)} %constant.26.clone.a, ...), custom_call_target="tpu_custom_call" | custom-call | tf_op jit(solution)/shard_map/spectrum_second/pallas_call | solution.py:295
  169.5 34.8 %all_to_all.7 = f32[128,16,128]{2,1,0:T(8,128)} custom-call(f32[128,16,128]{2,1,0:T(8,128)} %bitcast.17), custom_call_target="tpu_custom_call" | custom-call | tf_op jit(solution)/shard_map/all_to_all/pallas_call | solution.py:280
  204.3 3.6 %force_kernel.3.force = f32[32,4096]{1,0:T(8,128)} custom-call(f32[2048,128]{1,0:T(8,128)} %bitcast.20, bf16[768,256]{1,0:T(8,128)(2,1)} %constant.27.clone.inverse_right, f32[2,32,128]{2,1,0:T(8,128)} %constant.28.clone.b.twiddle, bf16[256,1536]{1,0:T(8,128)(2,1)} %constant.23.clone.z_last), custom_call_target="tpu_custom_call" | custom-call | tf_op jit(solution)/shard_map/force_kernel/pallas_call | solution.py:295
  207.9 2.6 %collective-permute-start.1 = (f32[32,4096]{1,0:T(8,128)}, f32[32,4096]{1,0:T(8,128)S(1)}, u32[]{:S(2)}, u32[]{:S(2)}) collective-permute-start(f32[32,4096]{1,0:T(8,128)} %force_kernel.3.force), channel_id=1, source_target_pairs={{0,128},{128,0},{1,129},{129,1},{2,130},{130,2},{3,131},{131,3},{4... | collective-permute-start | bytes 1572872 | tf_op jit(solution)/shard_map/ppermute | solution.py:370
  210.6 12.2 %collective-permute-done.1.other = f32[32,4096]{1,0:T(8,128)S(1)} collective-permute-done((f32[32,4096]{1,0:T(8,128)}, f32[32,4096]{1,0:T(8,128)S(1)}, u32[]{:S(2)}, u32[]{:S(2)}) %collective-permute-start.1) | collective-permute-done | bytes 524320 | tf_op jit(solution)/shard_map/ppermute | solution.py:370
  222.8 0.0 copy-start.1
  222.8 0.8 copy-done.1
  223.5 8.5 %last_friction.1 = (f32[32,4096]{1,0:T(8,128)}, f32[32,4096]{1,0:T(8,128)}, f32[32,4096]{1,0:T(8,128)}) custom-call(f32[2]{0:T(128)} %impedance.3, f32[32,4096]{1,0:T(8,128)} %force_kernel.3.force, f32[32,4096]{1,0:T(8,128)} %copy-done.1, f32[32,4096]{1,0:T(8,128)} %prestress.3, f32[32,4096]{1,0:T(8,128)} %strength.3, f32[32,4096]{1,0:T(8,128)} %get-tuple-element.13.state), custom_call_target="tpu_custom_call" | custom-call | tf_op jit(solution)/shard_map/last_friction/pallas_call | solution.py:295
Async XLA Ops:
  94.5 14.8 %collective-permute-start = (f32[32,4096]{1,0:T(8,128)}, f32[32,4096]{1,0:T(8,128)S(1)}, u32[]{:S(2)}, u32[]{:S(2)}) collective-permute-start(f32[32,4096]{1,0:T(8,128)} %force_kernel.2.force), channel_id=1, source_target_pairs={{0,128},{128,0},{1,129},{129,1},{2,130},{130,2},{3,131},{131,3},{4... | collective-permute-start | bytes 1572872 | tf_op jit(solution)/shard_map/ppermute | solution.py:370
  109.4 0.8 copy-start
  207.9 14.8 %collective-permute-start.1 = (f32[32,4096]{1,0:T(8,128)}, f32[32,4096]{1,0:T(8,128)S(1)}, u32[]{:S(2)}, u32[]{:S(2)}) collective-permute-start(f32[32,4096]{1,0:T(8,128)} %force_kernel.3.force), channel_id=1, source_target_pairs={{0,128},{128,0},{1,129},{129,1},{2,130},{130,2},{3,131},{131,3},{4... | collective-permute-start | bytes 1572872 | tf_op jit(solution)/shard_map/ppermute | solution.py:370
  222.8 0.8 copy-start.1
where the time goes:
time: 232 us
  Pallas kernels  200 us (86%)
  waiting for transfers between devices  24.4 us (11%)
  starting transfers between devices  5.21 us (2%)
    pallas_call x4, Pallas kernels, all_to_all(): pl.pallas_call(exchange, out_shape=jax.ShapeDtypeStruct(shaped.shape, F32...  144 us
    pallas_call x7, Pallas kernels, call(): pl.pallas_call(body, out_shape=outs, in_specs=[whole(pltpu.SMEM if i in s...  56.4 us
    ppermute x2, waiting for transfers between devices, local(): other = lax.ppermute(force, 'side', [(0, 1), (1, 0)])  24.4 us
    ppermute x2, starting transfers between devices, local(): other = lax.ppermute(force, 'side', [(0, 1), (1, 0)])  5.21 us
  transfers between devices with their start and end apart: 2, of which 2 were waited for; matrix products, arithmetic and copies ran while one was open for 0% of the time, Pallas kernels for 0%

commit v1 on v0

v1 whole, which is shorter than its diff:
```python
import functools
import math

import jax
import jax.numpy as jnp
import ml_dtypes
import numpy as np
from jax import lax
from jax.experimental import pallas as pl
from jax.experimental.pallas import tpu as pltpu
from jax.sharding import PartitionSpec as P

NX = 4096
NZ = 4096
LAGS = 8
NEWTON = 4
STEPS = 2
SLABS = 128
ROWS = 32
LANES = 128
MESH = pl.DeviceIdType.MESH
F32 = jnp.float32
BF16 = jnp.bfloat16
VMEM_BYTES = 56 * 2**20


def high_low(table, axis):
    table = table.astype(np.float32)
    high = table.astype(ml_dtypes.bfloat16)
    low = (table - high.astype(np.float32)).astype(ml_dtypes.bfloat16)
    return np.concatenate([high, low, high], axis=axis)


def complex_matrix(count, sign):
    angle = 2.0 * math.pi / count * (np.outer(np.arange(count), np.arange(count)) % count)
    cos, sin = np.cos(angle), sign * np.sin(angle)
    return np.block([[cos, -sin], [sin, cos]])


def tables():
    forward, inverse = complex_matrix(128, -1.0), complex_matrix(128, 1.0)
    forward_32 = complex_matrix(32, -1.0).reshape(2, 32, 2, 32)
    inverse_32 = complex_matrix(32, 1.0).reshape(2, 32, 2, 32)
    eye = np.eye(8)
    z_first = np.einsum("ajn,xy->ajxny", forward_32[:, :, 0], eye).reshape(512, 256)
    x_second = np.einsum("akcgx,ij->akicgjx", forward_32.reshape(2, 32, 2, 4, 8), eye).reshape(512, 512)
    x_third = np.einsum("axck,ij->axickj", inverse_32, eye).reshape(512, 512)
    z_last = np.einsum("zcgj,xy->zxcgyj", inverse_32[0].reshape(32, 2, 4, 8), eye).reshape(256, 512) / (NX * NZ)
    phase = 2.0 * math.pi / 4096 * np.outer(np.arange(32), np.arange(128))
    twiddle = np.stack([np.cos(phase), np.sin(phase)]).astype(np.float32)
    return dict(
        z_first=high_low(z_first, 1),
        x_second=high_low(x_second, 1),
        x_third=high_low(x_third, 1),
        z_last=high_low(z_last, 1),
        forward_left=high_low(forward, 1),
        inverse_left=high_low(inverse, 1),
        forward_right=high_low(forward.T, 0),
        inverse_right=high_low(inverse.T, 0),
        twiddle=twiddle,
        twiddle_rows=np.repeat(twiddle, 8, axis=1),
    )


def split(value):
    high = value.astype(BF16)
    low = (value - high.astype(F32)).astype(BF16)
    return high, low


def left_product(table, value):
    high, low = split(value)
    stacked = jnp.concatenate([high, high, low], axis=0)
    return jnp.dot(table, stacked, preferred_element_type=F32)


def right_product(value, table):
    high, low = split(value)
    stacked = jnp.concatenate([high, high, low], axis=1)
    return jnp.dot(stacked, table, preferred_element_type=F32)


def left_product_transposed(table, value):
    high, low = split(value)
    stacked = jnp.concatenate([high, high, low], axis=1)
    return lax.dot_general(table, stacked, (((1,), (1,)), ((), ())), preferred_element_type=F32)


def turn(real, imag, cos, sin):
    return real * cos - imag * sin, real * sin + imag * cos


def put_group(chunks, fixed, value, by_half):
    for part in range(2):
        for half in range(2):
            chunk, rows = by_half(half)
            piece = value[part * 128 : part * 128 + 128, half * 128 : half * 128 + 128]
            chunks[chunk, pl.ds(rows * 4 + part * 2 + fixed, SLABS, stride=8), :] = piece


def get_pair(chunks, chunk, rows):
    return jnp.concatenate(
        [
            jnp.concatenate(
                [chunks[chunk, pl.ds(rows * 4 + part * 2 + q, SLABS, stride=8), :] for q in range(2)], axis=1
            )
            for part in range(2)
        ],
        axis=0,
    )


def z_forward(field, rows, send, t):
    cos, sin = t["twiddle_rows"][0], t["twiddle_rows"][1]
    columns = [
        jnp.concatenate(
            [field[group * 8 : group * 8 + 8, n * 128 : n * 128 + 128] for n in range(32)], axis=0
        )
        for group in (2 * rows, 2 * rows + 1)
    ]
    first = left_product(t["z_first"][...], jnp.concatenate(columns, axis=1))
    for q in range(2):
        piece = first[:, q * 128 : q * 128 + 128]
        real, imag = turn(piece[:256], piece[256:], cos, -sin)
        turned = jnp.concatenate([real, imag], axis=1)
        result = left_product_transposed(t["forward_left"][...], turned)
        put_group(send, q, result, lambda half: (half, rows))


def gather_stage(pieces, table, twiddle, sign, middle):
    for pair, piece in enumerate(pieces):
        first = right_product(piece().T, table[...])
        cos = twiddle[0, pair * 16 : pair * 16 + 16, :].reshape(2, 1, 8, 128)
        sin = sign * twiddle[1, pair * 16 : pair * 16 + 16, :].reshape(2, 1, 8, 128)
        real, imag = turn(
            first[:, :128].reshape(2, 16, 8, 128), first[:, 128:].reshape(2, 16, 8, 128), cos, sin
        )
        middle[0, 2 * pair : 2 * pair + 2] = real.reshape(2, 128, 128)
        middle[1, 2 * pair : 2 * pair + 2] = imag.reshape(2, 128, 128)


def middle_columns(middle):
    return jnp.concatenate(
        [
            jnp.concatenate(
                [middle[c, g, q * 64 : q * 64 + 64, :] for c in range(2) for g in range(4)], axis=0
            )
            for q in range(2)
        ],
        axis=1,
    )


def past_sums(kernel, history, sums):
    def add(k, carry):
        lanes = pl.ds(pl.multiple_of(k * 128, 128), 128)
        for pair in range(2):
            rows = slice(pair * 16, pair * 16 + 16)
            weights = [kernel[lag, rows, lanes].astype(F32) for lag in range(1, LAGS + 1)]
            for part in range(2):
                past = [history[lag, part, rows, lanes].astype(F32) for lag in range(LAGS)]
                first = weights[0] * past[0]
                for lag in range(1, LAGS):
                    first = first + weights[lag] * past[lag]
                second = weights[1] * past[0]
                for lag in range(2, LAGS):
                    second = second + weights[lag] * past[lag - 1]
                sums[0, part, rows, lanes] = first
                sums[1, part, rows, lanes] = second
        return carry

    lax.fori_loop(0, 32, add, 0)


def spectrum_phase(step, chunk, received, kernel, sums, send, t, middle, wide):
    gather_stage(
        [functools.partial(get_pair, received, chunk, rows) for rows in range(2)],
        t["forward_right"], t["twiddle"], -1.0, middle,
    )
    cos, sin = t["twiddle_rows"][0], t["twiddle_rows"][1]
    wide[...] = left_product(t["x_second"][...], middle_columns(middle))
    rows = slice(chunk * 16, chunk * 16 + 16)

    def convolve(k, carry):
        lanes = pl.ds(pl.multiple_of(k * 128, 128), 128)
        newest = kernel[0, rows, lanes].astype(F32)
        next_newest = kernel[1, rows, lanes].astype(F32)
        for part in range(2):
            place = pl.ds(pl.multiple_of(part * 256 + k * 8, 8), 8)
            fresh = wide[place, :]
            rounded = jnp.concatenate([fresh[:, :128], fresh[:, 128:]], axis=0).astype(BF16).astype(F32)
            total = newest * rounded + sums[step, part, rows, lanes]
            if step + 1 < STEPS:
                sums[step + 1, part, rows, lanes] = sums[step + 1, part, rows, lanes] + next_newest * rounded
            wide[place, :] = jnp.concatenate([total[:8], total[8:]], axis=1)
        return carry

    lax.fori_loop(0, 32, convolve, 0)
    third = left_product(t["x_third"][...], wide[...])
    for q in range(2):
        piece = third[:, q * 128 : q * 128 + 128]
        real, imag = turn(piece[:256], piece[256:], cos, sin)
        turned = jnp.concatenate([real, imag], axis=1)
        result = left_product_transposed(t["inverse_left"][...], turned)
        put_group(send, q, result, lambda half: (chunk, half))


def z_inverse(received, rows, force, t, middle):
    gather_stage(
        [functools.partial(get_pair, received, chunk, rows) for chunk in range(2)],
        t["inverse_right"], t["twiddle"], 1.0, middle,
    )
    last = left_product(t["z_last"][...], middle_columns(middle))
    for q in range(2):
        group = 2 * rows + q
        for n in range(32):
            force[group * 8 : group * 8 + 8, n * 128 : n * 128 + 128] = last[
                n * 8 : n * 8 + 8, q * 128 : q * 128 + 128
            ]


def friction(rows, is_first, impedance, force, other, prestress, strength, state, speed, rate_out):
    eta_first, eta_second = impedance[0], impedance[1]
    eta_total = eta_first + eta_second
    weight_first = eta_second / eta_total
    weight_second = eta_first / eta_total
    eta_joint = eta_first * eta_second / eta_total
    own_weight = jnp.where(is_first, weight_first, weight_second)
    other_weight = jnp.where(is_first, weight_second, weight_first)
    own_scale = jnp.where(is_first, 1.0 / eta_first, -1.0 / eta_second)

    def solve(index, carry):
        row = rows * 16 + pl.multiple_of(lax.rem(index, 2) * 8, 8)
        lane = pl.multiple_of(lax.div(index, 2) * 512, 512)
        at = (pl.ds(row, 8), pl.ds(lane, 512))
        own = force[at]
        stress_now = prestress[at]
        normal = strength[at]
        psi = state[at]
        locked = stress_now + (own_weight * own + other_weight * other[at])
        rate = locked / (eta_joint + normal)
        factor = 0.5 * jnp.exp(psi)
        normal_factor = normal * factor
        for _ in range(NEWTON):
            scaled = factor * rate
            magnitude = jnp.abs(scaled)
            square = magnitude * magnitude
            root = jnp.sqrt(1.0 + square)
            arc = jnp.log1p(magnitude + square / (1.0 + root))
            arc = jnp.where(scaled < 0.0, -arc, arc)
            misfit = normal * arc + eta_joint * rate - locked
            slope = normal_factor / root + eta_joint
            rate = rate - 0.5 * misfit / slope
        stress = locked - eta_joint * rate
        speed[at] = (stress_now + own - stress) * own_scale
        rate_out[at] = rate
        state[at] = psi + 0.25 * (jnp.exp(-psi) - jnp.abs(rate))
        return carry

    lax.fori_loop(0, 16, solve, 0)


TABLES = (
    "z_first", "forward_left", "twiddle_rows", "forward_right", "twiddle",
    "x_second", "x_third", "inverse_left", "inverse_right", "z_last",
)
FIELDS = ("velocity", "kernel", "history", "prestress", "strength", "state")


def simulate(*refs):
    count = len(TABLES) + len(FIELDS)
    impedance = refs[0]
    outside = refs[1 : 1 + count]
    speed_out, rate_out, state_out = refs[1 + count : 4 + count]
    inside = refs[4 + count : 4 + 2 * count]
    (send, recv, middle, wide, sums, force, other,
     load_sem, own_sem, send_sem, recv_sem, side_send_sem, side_recv_sem) = refs[4 + 2 * count :]
    names = FIELDS[:1] + TABLES[:3] + FIELDS[1:3] + TABLES[3:] + FIELDS[3:]
    t = dict(zip(names, inside))
    me = lax.axis_index("slab")
    side = lax.axis_index("side")
    barrier = pltpu.get_barrier_semaphore()

    def greet(i, carry):
        there = lax.rem(me + i, SLABS)
        pl.semaphore_signal(barrier, inc=1, device_id=(side, there), device_id_type=MESH)
        return carry

    pl.semaphore_signal(barrier, inc=1, device_id=(1 - side, me), device_id_type=MESH)
    lax.fori_loop(1, SLABS, greet, 0)

    loads = {
        name: pltpu.make_async_copy(outside[k], inside[k], load_sem.at[k]) for k, name in enumerate(names)
    }
    for name in names:
        loads[name].start()

    def need(*wanted):
        for name in wanted:
            loads.pop(name).wait()

    def start(stage, chunk):
        def one(i, carry):
            there = lax.rem(me + i, SLABS)
            pltpu.make_async_remote_copy(
                src_ref=send.at[stage, chunk, pl.ds(pl.multiple_of(there * 8, 8), 8)],
                dst_ref=recv.at[stage, chunk, pl.ds(pl.multiple_of(me * 8, 8), 8)],
                send_sem=send_sem.at[stage, chunk],
                recv_sem=recv_sem.at[stage, chunk],
                device_id=(side, there),
                device_id_type=MESH,
            ).start()
            return carry

        lax.fori_loop(1, SLABS, one, 0)
        own(stage, chunk).start()

    def own(stage, chunk):
        mine = pl.ds(pl.multiple_of(me * 8, 8), 8)
        return pltpu.make_async_copy(
            send.at[stage, chunk, mine], recv.at[stage, chunk, mine], own_sem.at[stage, chunk]
        )

    def arrived(stage, chunk):
        own(stage, chunk).wait()
        bulk = recv.at[stage, chunk, pl.ds(0, (SLABS - 1) * 8)]
        pltpu.make_async_copy(bulk, bulk, recv_sem.at[stage, chunk]).wait()

    def left(stage, chunk):
        bulk = send.at[stage, chunk, pl.ds(0, (SLABS - 1) * 8)]
        pltpu.make_async_copy(bulk, bulk, send_sem.at[stage, chunk]).wait()

    def across(step, rows):
        place = pl.ds(rows * 16, 16)
        return pltpu.make_async_remote_copy(
            src_ref=force.at[step, place],
            dst_ref=other.at[step, place],
            send_sem=side_send_sem.at[step, rows],
            recv_sem=side_recv_sem.at[step, rows],
            device_id=(1 - side, me),
            device_id_type=MESH,
        )

    need("velocity", "z_first", "forward_left", "twiddle_rows")
    for rows in range(2):
        z_forward(t["velocity"], rows, send.at[0], t)
    pl.semaphore_wait(barrier, SLABS)
    for chunk in range(2):
        start(0, chunk)
    need("kernel", "history")
    past_sums(t["kernel"], t["history"], sums)
    need(*tuple(loads))
    for step in range(STEPS):
        there, back = 2 * step, 2 * step + 1
        for chunk in range(2):
            arrived(there, chunk)
            spectrum_phase(step, chunk, recv.at[there], t["kernel"], sums, send.at[back], t, middle, wide)
            start(back, chunk)
        for chunk in range(2):
            arrived(back, chunk)
        for rows in range(2):
            z_inverse(recv.at[back], rows, force.at[step], t, middle)
            across(step, rows).start()
        for rows in range(2):
            across(step, rows).wait_recv()
            last = step == STEPS - 1
            friction(
                rows, side == 0, impedance, force.at[step], other.at[step], t["prestress"], t["strength"],
                t["state"], speed_out if last else t["velocity"], rate_out,
            )
            if not last:
                z_forward(t["velocity"], rows, send.at[2 * step + 2], t)
        if not last:
            for chunk in range(2):
                start(2 * step + 2, chunk)
    state_out[...] = t["state"][...]
    for stage in range(2 * STEPS):
        for chunk in range(2):
            left(stage, chunk)
    for step in range(STEPS):
        for rows in range(2):
            across(step, rows).wait_send()


def whole(space=pltpu.VMEM):
    return pl.BlockSpec(memory_space=space)


def local(t, velocity, kernel, history, impedance, prestress, strength, fault_state):
    given = dict(
        t,
        velocity=velocity[0], kernel=kernel[0], history=history[0],
        prestress=prestress, strength=strength, state=fault_state,
    )
    names = FIELDS[:1] + TABLES[:3] + FIELDS[1:3] + TABLES[3:] + FIELDS[3:]
    values = [given[name] for name in names]
    field = jax.ShapeDtypeStruct((ROWS, NZ), F32)
    semaphores = pltpu.SemaphoreType.DMA
    speed, rate, state = pl.pallas_call(
        simulate,
        out_shape=(field, field, field),
        in_specs=[whole(pltpu.SMEM)] + [whole(pl.ANY)] * len(values),
        out_specs=(whole(), whole(), whole()),
        scratch_shapes=[pltpu.VMEM(v.shape, v.dtype) for v in values]
        + [
            pltpu.VMEM((2 * STEPS, 2, SLABS * 8, LANES), F32),
            pltpu.VMEM((2 * STEPS, 2, SLABS * 8, LANES), F32),
            pltpu.VMEM((2, 4, 128, LANES), F32),
            pltpu.VMEM((512, 256), F32),
            pltpu.VMEM((STEPS, 2, ROWS, NX), F32),
            pltpu.VMEM((STEPS, ROWS, NZ), F32),
            pltpu.VMEM((STEPS, ROWS, NZ), F32),
            semaphores((len(values),)),
            semaphores((2 * STEPS, 2)),
            semaphores((2 * STEPS, 2)),
            semaphores((2 * STEPS, 2)),
            semaphores((STEPS, 2)),
            semaphores((STEPS, 2)),
        ],
        compiler_params=pltpu.CompilerParams(
            collective_id=0, has_side_effects=True, vmem_limit_bytes=VMEM_BYTES
        ),
        name="simulate",
    )(impedance, *values)
    return (speed[None], rate, state)


def solution(mesh):
    placed = (
        P("side", "slab", None),
        P("side", None, "slab", None),
        P("side", None, None, "slab", None),
        P(),
        P("slab", None),
        P("slab", None),
        P("slab", None),
    )
    constants = tables()

    def run(*args):
        return local({name: jnp.asarray(value) for name, value in constants.items()}, *args)

    return jax.shard_map(
        run,
        mesh=mesh,
        in_specs=placed,
        out_specs=(P("side", "slab", None), P("slab", None), P("slab", None)),
        check_vma=False,
    )
```

time: 232 us -> 153 us (0.66)
  Pallas kernels: 200 us -> 148 us
  waiting for transfers between devices: 24.4 us -> 0 us
  starting transfers between devices: 5.21 us -> 0 us
  local copies, waits for them, and re-layouts: 1.59 us -> 4.59 us
    pallas_call x11 -> x1, Pallas kernels: 200 us -> 148 us  [local(): pl.pallas_call(simulate, out_shape=(field, field, field), in_specs=[whole...]
    ppermute x2 -> x0, waiting for transfers between devices: 24.4 us -> none  [local(): other = lax.ppermute(force, 'side', [(0, 1), (1, 0)])]
    ppermute x2 -> x0, starting transfers between devices: 5.21 us -> none  [local(): other = lax.ppermute(force, 'side', [(0, 1), (1, 0)])]
    unnamed x4 -> x5, local copies, waits for them, and re-layouts: 1.59 us -> 4.59 us
  transfers between devices with their start and end apart: 2 -> 0, of which waited for: 2 -> 0; matrix products, arithmetic and copies ran while one was open for 0% -> 0% of each run, Pallas kernels for 0% -> 0%
where the time goes in v1:
time: 153 us
  Pallas kernels  148 us (97%)
  local copies, waits for them, and re-layouts  4.59 us (3%)
    pallas_call x1, Pallas kernels, local(): pl.pallas_call(simulate, out_shape=(field, field, field), in_specs=[whole...  148 us
    unnamed x5, local copies, waits for them, and re-layouts  4.59 us

profile of v1, /device:TPU:1, one launch (start us, length us, event | category | flops | bytes accessed | tf_op | source)
XLA Modules:
  0.0 153.3 jit_solution(9695036721049258285)
XLA Ops:
  0.6 148.1 %simulate.1 = (f32[32,4096]{1,0:T(8,128)}, f32[32,4096]{1,0:T(8,128)}, f32[32,4096]{1,0:T(8,128)}) custom-call(f32[2]{0:T(128)} %refs_0_.1, f32[32,4096]{1,0:T(8,128)} %bitcast.6, bf16[512,768]{1,0:T(8,128)(2,1)} %constant.20.clone.refs_2_, bf16[256,768]{1,0:T(8,128)(2,1)} %constant.24.clone.refs_3_, f32[2,256,128]{2,1,0:T(8,128)} %constant.29.clone.refs_4_, ...), custom_call_target="tpu_custom_call" | custom-call | tf_op jit(solution)/shard_map/simulate/pallas_call | solution.py:399
  148.7 0.0 copy-start
  148.7 1.9 %copy.23 = f32[1,32,4096]{2,1,0:T(8,128)} copy(f32[1,32,4096]{2,1,0:T(8,128)} %bitcast.7) | data formatting | bytes 1048576
  150.7 1.9 %copy.24 = f32[32,4096]{1,0:T(8,128)} copy(f32[32,4096]{1,0:T(8,128)} %get-tuple-element.13) | data formatting | bytes 1048576
  152.5 0.0 copy-done
  152.5 0.8 copy.25
Async XLA Ops:
  148.7 3.8 %copy-start = (f32[32,4096]{1,0:T(8,128)S(1)}, f32[32,4096]{1,0:T(8,128)}, u32[]{:S(2)}) copy-start(f32[32,4096]{1,0:T(8,128)} %get-tuple-element.14) | copy-start | bytes 1572868

commit v2 on v1

--- a/solution.py
+++ b/solution.py
@@ -21,7 +21,7 @@
 MESH = pl.DeviceIdType.MESH
 F32 = jnp.float32
 BF16 = jnp.bfloat16
-VMEM_BYTES = 56 * 2**20
+VMEM_BYTES = 40 * 2**20
 
 
 def high_low(table, axis):
@@ -90,19 +90,24 @@
     return real * cos - imag * sin, real * sin + imag * cos
 
 
+def flat(chunks, chunk):
+    return chunks.at[chunk].reshape(SLABS * 8, LANES)
+
+
 def put_group(chunks, fixed, value, by_half):
     for part in range(2):
         for half in range(2):
             chunk, rows = by_half(half)
             piece = value[part * 128 : part * 128 + 128, half * 128 : half * 128 + 128]
-            chunks[chunk, pl.ds(rows * 4 + part * 2 + fixed, SLABS, stride=8), :] = piece
+            flat(chunks, chunk)[pl.ds(rows * 4 + part * 2 + fixed, SLABS, stride=8), :] = piece
 
 
 def get_pair(chunks, chunk, rows):
+    ref = flat(chunks, chunk)
     return jnp.concatenate(
         [
             jnp.concatenate(
-                [chunks[chunk, pl.ds(rows * 4 + part * 2 + q, SLABS, stride=8), :] for q in range(2)], axis=1
+                [ref[pl.ds(rows * 4 + part * 2 + q, SLABS, stride=8), :] for q in range(2)], axis=1
             )
             for part in range(2)
         ],
@@ -195,7 +200,7 @@
             wide[place, :] = jnp.concatenate([total[:8], total[8:]], axis=1)
         return carry
 
-    lax.fori_loop(0, 32, convolve, 0)
+    lax.fori_loop(0, 32, convolve, 0, unroll=2)
     third = left_product(t["x_third"][...], wide[...])
     for q in range(2):
         piece = third[:, q * 128 : q * 128 + 128]
@@ -243,14 +248,11 @@
         normal_factor = normal * factor
         for _ in range(NEWTON):
             scaled = factor * rate
-            magnitude = jnp.abs(scaled)
-            square = magnitude * magnitude
-            root = jnp.sqrt(1.0 + square)
-            arc = jnp.log1p(magnitude + square / (1.0 + root))
+            root = jnp.sqrt(1.0 + scaled * scaled)
+            arc = jnp.log(jnp.abs(scaled) + root)
             arc = jnp.where(scaled < 0.0, -arc, arc)
             misfit = normal * arc + eta_joint * rate - locked
-            slope = normal_factor / root + eta_joint
-            rate = rate - 0.5 * misfit / slope
+            rate = rate - 0.5 * misfit * root / (normal_factor + eta_joint * root)
         stress = locked - eta_joint * rate
         speed[at] = (stress_now + own - stress) * own_scale
         rate_out[at] = rate
@@ -286,49 +288,59 @@
         pl.semaphore_signal(barrier, inc=1, device_id=(side, there), device_id_type=MESH)
         return carry
 
-    pl.semaphore_signal(barrier, inc=1, device_id=(1 - side, me), device_id_type=MESH)
-    lax.fori_loop(1, SLABS, greet, 0)
-
     loads = {
         name: pltpu.make_async_copy(outside[k], inside[k], load_sem.at[k]) for k, name in enumerate(names)
     }
-    for name in names:
+    for name in names[:4]:
         loads[name].start()
+    pl.semaphore_signal(barrier, inc=1, device_id=(1 - side, me), device_id_type=MESH)
+    lax.fori_loop(1, SLABS, greet, 0, unroll=4)
 
     def need(*wanted):
         for name in wanted:
             loads.pop(name).wait()
 
-    def start(stage, chunk):
+    def place(name, where):
+        return {
+            "first rows": (slice(None), where, pl.ds(0, 4)),
+            "first waves": (0, where),
+            "mixed": (0, where, pl.ds(4, 4)) if name[0] == "out" else (1, where, pl.ds(0, 4)),
+            "last": (1, where, pl.ds(4, 4)),
+        }[name[1]]
+
+    def own(stage, name, index):
+        mine = place(name, me)
+        return pltpu.make_async_copy(
+            send.at[(stage,) + mine], recv.at[(stage,) + mine], own_sem.at[stage, index]
+        )
+
+    def start(stage, name, index):
         def one(i, carry):
             there = lax.rem(me + i, SLABS)
             pltpu.make_async_remote_copy(
-                src_ref=send.at[stage, chunk, pl.ds(pl.multiple_of(there * 8, 8), 8)],
-                dst_ref=recv.at[stage, chunk, pl.ds(pl.multiple_of(me * 8, 8), 8)],
-                send_sem=send_sem.at[stage, chunk],
-                recv_sem=recv_sem.at[stage, chunk],
+                src_ref=send.at[(stage,) + place(name, there)],
+                dst_ref=recv.at[(stage,) + place(name, me)],
+                send_sem=send_sem.at[stage, index],
+                recv_sem=recv_sem.at[stage, index],
                 device_id=(side, there),
                 device_id_type=MESH,
             ).start()
             return carry
 
-        lax.fori_loop(1, SLABS, one, 0)
-        own(stage, chunk).start()
-
-    def own(stage, chunk):
-        mine = pl.ds(pl.multiple_of(me * 8, 8), 8)
-        return pltpu.make_async_copy(
-            send.at[stage, chunk, mine], recv.at[stage, chunk, mine], own_sem.at[stage, chunk]
-        )
-
-    def arrived(stage, chunk):
-        own(stage, chunk).wait()
-        bulk = recv.at[stage, chunk, pl.ds(0, (SLABS - 1) * 8)]
-        pltpu.make_async_copy(bulk, bulk, recv_sem.at[stage, chunk]).wait()
-
-    def left(stage, chunk):
-        bulk = send.at[stage, chunk, pl.ds(0, (SLABS - 1) * 8)]
-        pltpu.make_async_copy(bulk, bulk, send_sem.at[stage, chunk]).wait()
+        lax.fori_loop(1, SLABS, one, 0, unroll=4)
+        own(stage, name, index).start()
+
+    def arrived(stage, name, index):
+        own(stage, name, index).wait()
+        bulk = recv.at[(stage,) + place(name, pl.ds(0, SLABS - 1))]
+        pltpu.make_async_copy(bulk, bulk, recv_sem.at[stage, index]).wait()
+
+    def left(stage, name, index):
+        bulk = send.at[(stage,) + place(name, pl.ds(0, SLABS - 1))]
+        pltpu.make_async_copy(bulk, bulk, send_sem.at[stage, index]).wait()
+
+    out_names = [("out", "first rows"), ("out", "mixed"), ("out", "last")]
+    back_names = [("back", "first waves"), ("back", "mixed"), ("back", "last")]
 
     def across(step, rows):
         place = pl.ds(rows * 16, 16)
@@ -341,45 +353,61 @@
             device_id_type=MESH,
         )
 
-    need("velocity", "z_first", "forward_left", "twiddle_rows")
-    for rows in range(2):
-        z_forward(t["velocity"], rows, send.at[0], t)
+    def send_rows(stage, rows):
+        if rows == 0:
+            start(stage, out_names[0], 0)
+        else:
+            start(stage, out_names[1], 1)
+            start(stage, out_names[2], 2)
+
+    need(*names[:4])
+    for name in names[4:]:
+        loads[name].start()
+    z_forward(t["velocity"], 0, send.at[0], t)
     pl.semaphore_wait(barrier, SLABS)
-    for chunk in range(2):
-        start(0, chunk)
+    send_rows(0, 0)
+    z_forward(t["velocity"], 1, send.at[0], t)
+    send_rows(0, 1)
     need("kernel", "history")
     past_sums(t["kernel"], t["history"], sums)
     need(*tuple(loads))
     for step in range(STEPS):
         there, back = 2 * step, 2 * step + 1
-        for chunk in range(2):
-            arrived(there, chunk)
-            spectrum_phase(step, chunk, recv.at[there], t["kernel"], sums, send.at[back], t, middle, wide)
-            start(back, chunk)
-        for chunk in range(2):
-            arrived(back, chunk)
+        last = step == STEPS - 1
+        arrived(there, out_names[0], 0)
+        arrived(there, out_names[1], 1)
+        spectrum_phase(step, 0, recv.at[there], t["kernel"], sums, send.at[back], t, middle, wide)
+        start(back, back_names[0], 0)
+        arrived(there, out_names[2], 2)
+        spectrum_phase(step, 1, recv.at[there], t["kernel"], sums, send.at[back], t, middle, wide)
+        start(back, back_names[1], 1)
+        start(back, back_names[2], 2)
+        arrived(back, back_names[0], 0)
         for rows in range(2):
+            arrived(back, back_names[1 + rows], 1 + rows)
             z_inverse(recv.at[back], rows, force.at[step], t, middle)
             across(step, rows).start()
         for rows in range(2):
             across(step, rows).wait_recv()
-            last = step == STEPS - 1
             friction(
                 rows, side == 0, impedance, force.at[step], other.at[step], t["prestress"], t["strength"],
                 t["state"], speed_out if last else t["velocity"], rate_out,
             )
             if not last:
                 z_forward(t["velocity"], rows, send.at[2 * step + 2], t)
-        if not last:
-            for chunk in range(2):
-                start(2 * step + 2, chunk)
+                send_rows(2 * step + 2, rows)
     state_out[...] = t["state"][...]
     for stage in range(2 * STEPS):
-        for chunk in range(2):
-            left(stage, chunk)
+        for index, name in enumerate(back_names if stage % 2 else out_names):
+            left(stage, name, index)
     for step in range(STEPS):
         for rows in range(2):
             across(step, rows).wait_send()
+
+
+def hand_over(*refs):
+    for source, target in zip(refs[:3], refs[3:]):
+        target[...] = source[...]
 
 
 def whole(space=pltpu.VMEM):
@@ -396,24 +424,24 @@
     values = [given[name] for name in names]
     field = jax.ShapeDtypeStruct((ROWS, NZ), F32)
     semaphores = pltpu.SemaphoreType.DMA
-    speed, rate, state = pl.pallas_call(
+    results = pl.pallas_call(
         simulate,
         out_shape=(field, field, field),
         in_specs=[whole(pltpu.SMEM)] + [whole(pl.ANY)] * len(values),
         out_specs=(whole(), whole(), whole()),
         scratch_shapes=[pltpu.VMEM(v.shape, v.dtype) for v in values]
         + [
-            pltpu.VMEM((2 * STEPS, 2, SLABS * 8, LANES), F32),
-            pltpu.VMEM((2 * STEPS, 2, SLABS * 8, LANES), F32),
+            pltpu.VMEM((2 * STEPS, 2, SLABS, 8, LANES), F32),
+            pltpu.VMEM((2 * STEPS, 2, SLABS, 8, LANES), F32),
             pltpu.VMEM((2, 4, 128, LANES), F32),
             pltpu.VMEM((512, 256), F32),
             pltpu.VMEM((STEPS, 2, ROWS, NX), F32),
             pltpu.VMEM((STEPS, ROWS, NZ), F32),
             pltpu.VMEM((STEPS, ROWS, NZ), F32),
             semaphores((len(values),)),
-            semaphores((2 * STEPS, 2)),
-            semaphores((2 * STEPS, 2)),
-            semaphores((2 * STEPS, 2)),
+            semaphores((2 * STEPS, 3)),
+            semaphores((2 * STEPS, 3)),
+            semaphores((2 * STEPS, 3)),
             semaphores((STEPS, 2)),
             semaphores((STEPS, 2)),
         ],
@@ -422,6 +450,14 @@
         ),
         name="simulate",
     )(impedance, *values)
+    speed, rate, state = pl.pallas_call(
+        hand_over,
+        out_shape=(field, field, field),
+        in_specs=[whole()] * 3,
+        out_specs=(whole(),) * 3,
+        compiler_params=pltpu.CompilerParams(vmem_limit_bytes=8 * 2**20),
+        name="hand_over",
+    )(*results)
     return (speed[None], rate, state)
 
 

time: 153 us -> 157 us (1.026)
  local copies, waits for them, and re-layouts: 4.59 us -> 17.2 us
  Pallas kernels: 148 us -> 139 us
    unnamed x5 -> x32, local copies, waits for them, and re-layouts: 4.59 us -> 17.2 us
    pallas_call x1, Pallas kernels: 148 us -> 137 us  [local(): pl.pallas_call(simulate, out_shape=(field, field, field), in_specs=[whole...]
where the time goes in v2:
time: 157 us
  Pallas kernels  139 us (89%)
  local copies, waits for them, and re-layouts  17.2 us (11%)
    pallas_call x1, Pallas kernels, local(): pl.pallas_call(simulate, out_shape=(field, field, field), in_specs=[whole...  137 us
    unnamed x32, local copies, waits for them, and re-layouts  17.2 us

profile of v2, /device:TPU:1, one launch (start us, length us, event | category | flops | bytes accessed | tf_op | source)
XLA Modules:
  0.0 156.6 jit_solution(9719070933613887020)
XLA Ops:
  0.6 0.0 copy-start
  0.6 1.7 %copy-done = bf16[1,9,32,4096]{3,2,1,0:T(8,128)(2,1)S(1)} copy-done((bf16[1,9,32,4096]{3,2,1,0:T(8,128)(2,1)S(1)}, bf16[1,9,32,4096]{3,2,1,0:T(8,128)(2,1)}, u32[]{:S(2)}) %copy-start) | copy-done | bytes 2359320
  2.3 0.0 copy-start.1
  2.3 1.4 copy-done.1
  3.7 0.0 copy-start.2
  3.7 1.4 copy-done.2
  5.1 0.0 copy-start.3
  5.1 1.1 copy-done.3
  6.2 0.0 copy-start.4
  6.3 1.1 copy-done.4
  7.4 0.0 copy-start.5
  7.4 1.0 copy-done.5
  8.4 0.0 copy-start.6
  8.4 1.0 copy-done.6
  9.5 0.0 copy-start.7
  9.5 1.0 copy-done.7
  10.5 0.0 copy-start.8
  10.5 1.0 copy-done.8
  11.6 0.0 copy-start.9
  11.6 1.0 copy-done.9
  12.5 0.0 copy-start.10
  12.6 1.0 copy-done.10
  13.5 0.0 copy-start.11
  13.5 1.0 copy-done.11
  14.5 0.0 copy-start.12
  14.5 1.0 copy-done.12
  15.5 0.0 copy-start.13
  15.5 0.9 copy-done.13
  16.5 0.0 copy-start.14
  16.5 0.8 copy-done.14
  17.2 0.0 copy-start.15
  17.2 0.7 copy-done.15
  17.9 137.5 %simulate.1 = (f32[32,4096]{1,0:T(8,128)S(1)}, f32[32,4096]{1,0:T(8,128)S(1)}, f32[32,4096]{1,0:T(8,128)S(1)}) custom-call(f32[2]{0:T(128)S(1)} %copy-done.15, f32[32,4096]{1,0:T(8,128)S(1)} %bitcast.5, bf16[512,768]{1,0:T(8,128)(2,1)S(1)} %copy-done.4, bf16[256,768]{1,0:T(8,128)(2,1)S(1)} %copy-done.12, f32[2,256,128]{2,1,0:T(8,128)S(1)} %copy-done.13, ...), custom_call_target="tpu_custom_call" | custom-call | tf_op jit(solution)/shard_map/simulate/pallas_call | solution.py:427
  155.4 1.2 hand_over.1
Async XLA Ops:
  0.6 1.7 %copy-start = (bf16[1,9,32,4096]{3,2,1,0:T(8,128)(2,1)S(1)}, bf16[1,9,32,4096]{3,2,1,0:T(8,128)(2,1)}, u32[]{:S(2)}) copy-start(bf16[1,9,32,4096]{3,2,1,0:T(8,128)(2,1)} %param.18) | copy-start | bytes 7077892
  2.3 1.4 copy-start.1
  3.7 1.4 copy-start.2
  5.1 1.1 copy-start.3
  6.2 1.1 copy-start.4
  7.4 1.0 copy-start.5
  8.4 1.0 copy-start.6
  9.5 1.0 copy-start.7
  10.5 1.0 copy-start.8
  11.6 1.0 copy-start.9
  12.5 1.0 copy-start.10
  13.5 1.0 copy-start.11
  14.5 1.0 copy-start.12
  15.5 0.9 copy-start.13
  16.5 0.8 copy-start.14
  17.2 0.7 copy-start.15

commit v3 on v2

--- a/solution.py
+++ b/solution.py
@@ -21,7 +21,7 @@
 MESH = pl.DeviceIdType.MESH
 F32 = jnp.float32
 BF16 = jnp.bfloat16
-VMEM_BYTES = 40 * 2**20
+VMEM_BYTES = 56 * 2**20
 
 
 def high_low(table, axis):
@@ -94,20 +94,30 @@
     return chunks.at[chunk].reshape(SLABS * 8, LANES)
 
 
-def put_group(chunks, fixed, value, by_half):
+def turned_rows(real, imag):
+    return jnp.concatenate([real, imag], axis=1)
+
+
+def z_forward(field, group, send, t):
+    cos, sin = t["twiddle_rows"][0], t["twiddle_rows"][1]
+    rows = slice(group * 8, group * 8 + 8)
+    column = jnp.concatenate([field[rows, n * 128 : n * 128 + 128] for n in range(32)], axis=0)
+    first = left_product(t["z_first"][...], column)
+    real, imag = turn(first[:256], first[256:], cos, -sin)
+    result = left_product_transposed(t["forward_left"][...], turned_rows(real, imag))
     for part in range(2):
-        for half in range(2):
-            chunk, rows = by_half(half)
-            piece = value[part * 128 : part * 128 + 128, half * 128 : half * 128 + 128]
-            flat(chunks, chunk)[pl.ds(rows * 4 + part * 2 + fixed, SLABS, stride=8), :] = piece
-
-
-def get_pair(chunks, chunk, rows):
-    ref = flat(chunks, chunk)
+        for chunk in range(2):
+            flat(send, chunk)[pl.ds(group * 2 + part, SLABS, stride=8), :] = result[
+                part * 128 : part * 128 + 128, chunk * 128 : chunk * 128 + 128
+            ]
+
+
+def fetch(chunks, places):
     return jnp.concatenate(
         [
             jnp.concatenate(
-                [ref[pl.ds(rows * 4 + part * 2 + q, SLABS, stride=8), :] for q in range(2)], axis=1
+                [flat(chunks, chunk)[pl.ds(group * 2 + part, SLABS, stride=8), :] for chunk, group in places],
+                axis=1,
             )
             for part in range(2)
         ],
@@ -115,30 +125,14 @@
     )
 
 
-def z_forward(field, rows, send, t):
-    cos, sin = t["twiddle_rows"][0], t["twiddle_rows"][1]
-    columns = [
-        jnp.concatenate(
-            [field[group * 8 : group * 8 + 8, n * 128 : n * 128 + 128] for n in range(32)], axis=0
-        )
-        for group in (2 * rows, 2 * rows + 1)
-    ]
-    first = left_product(t["z_first"][...], jnp.concatenate(columns, axis=1))
-    for q in range(2):
-        piece = first[:, q * 128 : q * 128 + 128]
-        real, imag = turn(piece[:256], piece[256:], cos, -sin)
-        turned = jnp.concatenate([real, imag], axis=1)
-        result = left_product_transposed(t["forward_left"][...], turned)
-        put_group(send, q, result, lambda half: (half, rows))
-
-
-def gather_stage(pieces, table, twiddle, sign, middle):
-    for pair, piece in enumerate(pieces):
-        first = right_product(piece().T, table[...])
-        cos = twiddle[0, pair * 16 : pair * 16 + 16, :].reshape(2, 1, 8, 128)
-        sin = sign * twiddle[1, pair * 16 : pair * 16 + 16, :].reshape(2, 1, 8, 128)
+def x_stage(received, chunk, t, middle):
+    for pair in range(2):
+        rows = fetch(received, [(chunk, 2 * pair), (chunk, 2 * pair + 1)]).T
+        first = right_product(rows, t["forward_right"][...])
+        cos = t["twiddle"][0, pair * 16 : pair * 16 + 16, :].reshape(2, 1, 8, 128)
+        sin = t["twiddle"][1, pair * 16 : pair * 16 + 16, :].reshape(2, 1, 8, 128)
         real, imag = turn(
-            first[:, :128].reshape(2, 16, 8, 128), first[:, 128:].reshape(2, 16, 8, 128), cos, sin
+            first[:, :128].reshape(2, 16, 8, 128), first[:, 128:].reshape(2, 16, 8, 128), cos, -sin
         )
         middle[0, 2 * pair : 2 * pair + 2] = real.reshape(2, 128, 128)
         middle[1, 2 * pair : 2 * pair + 2] = imag.reshape(2, 128, 128)
@@ -178,10 +172,7 @@
 
 
 def spectrum_phase(step, chunk, received, kernel, sums, send, t, middle, wide):
-    gather_stage(
-        [functools.partial(get_pair, received, chunk, rows) for rows in range(2)],
-        t["forward_right"], t["twiddle"], -1.0, middle,
-    )
+    x_stage(received, chunk, t, middle)
     cos, sin = t["twiddle_rows"][0], t["twiddle_rows"][1]
     wide[...] = left_product(t["x_second"][...], middle_columns(middle))
     rows = slice(chunk * 16, chunk * 16 + 16)
@@ -202,29 +193,34 @@
 
     lax.fori_loop(0, 32, convolve, 0, unroll=2)
     third = left_product(t["x_third"][...], wide[...])
+    turned = []
     for q in range(2):
         piece = third[:, q * 128 : q * 128 + 128]
-        real, imag = turn(piece[:256], piece[256:], cos, sin)
-        turned = jnp.concatenate([real, imag], axis=1)
-        result = left_product_transposed(t["inverse_left"][...], turned)
-        put_group(send, q, result, lambda half: (chunk, half))
-
-
-def z_inverse(received, rows, force, t, middle):
-    gather_stage(
-        [functools.partial(get_pair, received, chunk, rows) for chunk in range(2)],
-        t["inverse_right"], t["twiddle"], 1.0, middle,
-    )
-    last = left_product(t["z_last"][...], middle_columns(middle))
-    for q in range(2):
-        group = 2 * rows + q
-        for n in range(32):
-            force[group * 8 : group * 8 + 8, n * 128 : n * 128 + 128] = last[
-                n * 8 : n * 8 + 8, q * 128 : q * 128 + 128
-            ]
-
-
-def friction(rows, is_first, impedance, force, other, prestress, strength, state, speed, rate_out):
+        turned.append(turned_rows(*turn(piece[:256], piece[256:], cos, sin)))
+    for pair in range(2):
+        places = [slice((2 * pair + g) * 64, (2 * pair + g) * 64 + 64) for g in range(2)]
+        ordered = jnp.concatenate([turned[q][place] for place in places for q in range(2)], axis=0)
+        result = left_product_transposed(t["inverse_left"][...], ordered)
+        for part in range(2):
+            for g in range(2):
+                flat(send, chunk)[pl.ds((2 * pair + g) * 2 + part, SLABS, stride=8), :] = result[
+                    part * 128 : part * 128 + 128, g * 128 : g * 128 + 128
+                ]
+
+
+def z_inverse(received, group, force, t):
+    rows = fetch(received, [(0, group), (1, group)]).T
+    first = right_product(rows, t["inverse_right"][...])
+    cos = t["twiddle"][0].reshape(4, 1, 8, 128)
+    sin = t["twiddle"][1].reshape(4, 1, 8, 128)
+    real, imag = turn(first[:, :128].reshape(4, 8, 8, 128), first[:, 128:].reshape(4, 8, 8, 128), cos, sin)
+    column = jnp.concatenate([real.reshape(256, 128), imag.reshape(256, 128)], axis=0)
+    last = left_product(t["z_last"][...], column)
+    for n in range(32):
+        force[group * 8 : group * 8 + 8, n * 128 : n * 128 + 128] = last[n * 8 : n * 8 + 8]
+
+
+def friction(group, is_first, impedance, force, other, prestress, strength, state, speed, rate_out):
     eta_first, eta_second = impedance[0], impedance[1]
     eta_total = eta_first + eta_second
     weight_first = eta_second / eta_total
@@ -235,9 +231,7 @@
     own_scale = jnp.where(is_first, 1.0 / eta_first, -1.0 / eta_second)
 
     def solve(index, carry):
-        row = rows * 16 + pl.multiple_of(lax.rem(index, 2) * 8, 8)
-        lane = pl.multiple_of(lax.div(index, 2) * 512, 512)
-        at = (pl.ds(row, 8), pl.ds(lane, 512))
+        at = (slice(group * 8, group * 8 + 8), pl.ds(pl.multiple_of(index * 512, 512), 512))
         own = force[at]
         stress_now = prestress[at]
         normal = strength[at]
@@ -259,7 +253,7 @@
         state[at] = psi + 0.25 * (jnp.exp(-psi) - jnp.abs(rate))
         return carry
 
-    lax.fori_loop(0, 16, solve, 0)
+    lax.fori_loop(0, 8, solve, 0)
 
 
 TABLES = (
@@ -301,12 +295,8 @@
             loads.pop(name).wait()
 
     def place(name, where):
-        return {
-            "first rows": (slice(None), where, pl.ds(0, 4)),
-            "first waves": (0, where),
-            "mixed": (0, where, pl.ds(4, 4)) if name[0] == "out" else (1, where, pl.ds(0, 4)),
-            "last": (1, where, pl.ds(4, 4)),
-        }[name[1]]
+        chunk, first, count = name
+        return (chunk, where) if count == 4 else (chunk, where, pl.ds(first * 2, count * 2))
 
     def own(stage, name, index):
         mine = place(name, me)
@@ -339,70 +329,69 @@
         bulk = send.at[(stage,) + place(name, pl.ds(0, SLABS - 1))]
         pltpu.make_async_copy(bulk, bulk, send_sem.at[stage, index]).wait()
 
-    out_names = [("out", "first rows"), ("out", "mixed"), ("out", "last")]
-    back_names = [("back", "first waves"), ("back", "mixed"), ("back", "last")]
+    both = slice(None)
+    out_names = [(both, 0, 1), (both, 1, 1), (0, 2, 1), (0, 3, 1), (1, 2, 2)]
+    back_names = [(0, 0, 4), (1, 0, 1), (1, 1, 1), (1, 2, 1), (1, 3, 1)]
 
     def across(step, rows):
-        place = pl.ds(rows * 16, 16)
+        lines = pl.ds(rows * 8, 8)
         return pltpu.make_async_remote_copy(
-            src_ref=force.at[step, place],
-            dst_ref=other.at[step, place],
+            src_ref=force.at[step, lines],
+            dst_ref=other.at[step, lines],
             send_sem=side_send_sem.at[step, rows],
             recv_sem=side_recv_sem.at[step, rows],
             device_id=(1 - side, me),
             device_id_type=MESH,
         )
 
-    def send_rows(stage, rows):
-        if rows == 0:
-            start(stage, out_names[0], 0)
-        else:
-            start(stage, out_names[1], 1)
-            start(stage, out_names[2], 2)
+    def send_rows(stage, group):
+        start(stage, out_names[group], group)
+        if group == 3:
+            start(stage, out_names[4], 4)
 
     need(*names[:4])
     for name in names[4:]:
         loads[name].start()
-    z_forward(t["velocity"], 0, send.at[0], t)
-    pl.semaphore_wait(barrier, SLABS)
-    send_rows(0, 0)
-    z_forward(t["velocity"], 1, send.at[0], t)
-    send_rows(0, 1)
+    for group in range(4):
+        z_forward(t["velocity"], group, send.at[0], t)
+        if group == 0:
+            pl.semaphore_wait(barrier, SLABS)
+        send_rows(0, group)
     need("kernel", "history")
     past_sums(t["kernel"], t["history"], sums)
     need(*tuple(loads))
     for step in range(STEPS):
         there, back = 2 * step, 2 * step + 1
         last = step == STEPS - 1
-        arrived(there, out_names[0], 0)
-        arrived(there, out_names[1], 1)
+        for index in range(4):
+            arrived(there, out_names[index], index)
         spectrum_phase(step, 0, recv.at[there], t["kernel"], sums, send.at[back], t, middle, wide)
         start(back, back_names[0], 0)
-        arrived(there, out_names[2], 2)
+        arrived(there, out_names[4], 4)
         spectrum_phase(step, 1, recv.at[there], t["kernel"], sums, send.at[back], t, middle, wide)
-        start(back, back_names[1], 1)
-        start(back, back_names[2], 2)
+        for group in range(4):
+            start(back, back_names[1 + group], 1 + group)
         arrived(back, back_names[0], 0)
-        for rows in range(2):
-            arrived(back, back_names[1 + rows], 1 + rows)
-            z_inverse(recv.at[back], rows, force.at[step], t, middle)
-            across(step, rows).start()
-        for rows in range(2):
-            across(step, rows).wait_recv()
+        for group in range(4):
+            arrived(back, back_names[1 + group], 1 + group)
+            z_inverse(recv.at[back], group, force.at[step], t)
+            across(step, group).start()
+        for group in range(4):
+            across(step, group).wait_recv()
             friction(
-                rows, side == 0, impedance, force.at[step], other.at[step], t["prestress"], t["strength"],
+                group, side == 0, impedance, force.at[step], other.at[step], t["prestress"], t["strength"],
                 t["state"], speed_out if last else t["velocity"], rate_out,
             )
             if not last:
-                z_forward(t["velocity"], rows, send.at[2 * step + 2], t)
-                send_rows(2 * step + 2, rows)
+                z_forward(t["velocity"], group, send.at[2 * step + 2], t)
+                send_rows(2 * step + 2, group)
     state_out[...] = t["state"][...]
     for stage in range(2 * STEPS):
         for index, name in enumerate(back_names if stage % 2 else out_names):
             left(stage, name, index)
     for step in range(STEPS):
-        for rows in range(2):
-            across(step, rows).wait_send()
+        for group in range(4):
+            across(step, group).wait_send()
 
 
 def hand_over(*refs):
@@ -439,11 +428,11 @@
             pltpu.VMEM((STEPS, ROWS, NZ), F32),
             pltpu.VMEM((STEPS, ROWS, NZ), F32),
             semaphores((len(values),)),
-            semaphores((2 * STEPS, 3)),
-            semaphores((2 * STEPS, 3)),
-            semaphores((2 * STEPS, 3)),
-            semaphores((STEPS, 2)),
-            semaphores((STEPS, 2)),
+            semaphores((2 * STEPS, 5)),
+            semaphores((2 * STEPS, 5)),
+            semaphores((2 * STEPS, 5)),
+            semaphores((STEPS, 4)),
+            semaphores((STEPS, 4)),
         ],
         compiler_params=pltpu.CompilerParams(
             collective_id=0, has_side_effects=True, vmem_limit_bytes=VMEM_BYTES
@@ -455,7 +444,7 @@
         out_shape=(field, field, field),
         in_specs=[whole()] * 3,
         out_specs=(whole(),) * 3,
-        compiler_params=pltpu.CompilerParams(vmem_limit_bytes=8 * 2**20),
+        compiler_params=pltpu.CompilerParams(vmem_limit_bytes=VMEM_BYTES),
         name="hand_over",
     )(*results)
     return (speed[None], rate, state)

time: 157 us -> 136 us (0.87)
  local copies, waits for them, and re-layouts: 17.2 us -> 0 us
  Pallas kernels: 139 us -> 135 us
    unnamed x32 -> x0, local copies, waits for them, and re-layouts: 17.2 us -> none
    pallas_call x1, Pallas kernels: 137 us -> 133 us  [local(): pl.pallas_call(simulate, out_shape=(field, field, field), in_specs=[whole...]
where the time goes in v3:
time: 136 us
  Pallas kernels  135 us (99%)
    pallas_call x1, Pallas kernels, local(): pl.pallas_call(simulate, out_shape=(field, field, field), in_specs=[whole...  133 us

profile of v3, /device:TPU:1, one launch (start us, length us, event | category | flops | bytes accessed | tf_op | source)
XLA Modules:
  0.0 136.1 jit_solution(13922218460590973614)
XLA Ops:
  0.6 132.9 %simulate.1 = (f32[32,4096]{1,0:T(8,128)}, f32[32,4096]{1,0:T(8,128)}, f32[32,4096]{1,0:T(8,128)}) custom-call(f32[2]{0:T(128)} %refs_0_.1, f32[32,4096]{1,0:T(8,128)} %bitcast.6, bf16[512,768]{1,0:T(8,128)(2,1)} %constant.20.clone.refs_2_, bf16[256,768]{1,0:T(8,128)(2,1)} %constant.24.clone.refs_3_, f32[2,256,128]{2,1,0:T(8,128)} %constant.29.clone.refs_4_, ...), custom_call_target="tpu_custom_call" | custom-call | tf_op jit(solution)/shard_map/simulate/pallas_call | solution.py:416
  133.5 2.5 %hand_over.1 = (f32[32,4096]{1,0:T(8,128)}, f32[32,4096]{1,0:T(8,128)}, f32[32,4096]{1,0:T(8,128)}) custom-call(f32[32,4096]{1,0:T(8,128)} %get-tuple-element.9.refs_0_, f32[32,4096]{1,0:T(8,128)} %get-tuple-element.10.refs_1_, f32[32,4096]{1,0:T(8,128)} %get-tuple-element.11.refs_2_), custom_call_target="tpu_custom_call" | custom-call | tf_op jit(solution)/shard_map/hand_over/pallas_call | solution.py:442

commit v4 on v3

--- a/solution.py
+++ b/solution.py
@@ -298,13 +298,16 @@
         chunk, first, count = name
         return (chunk, where) if count == 4 else (chunk, where, pl.ds(first * 2, count * 2))
 
-    def own(stage, name, index):
+    def own(stage, index):
+        name = messages[stage][index]
         mine = place(name, me)
         return pltpu.make_async_copy(
             send.at[(stage,) + mine], recv.at[(stage,) + mine], own_sem.at[stage, index]
         )
 
-    def start(stage, name, index):
+    def start(stage, index):
+        name = messages[stage][index]
+
         def one(i, carry):
             there = lax.rem(me + i, SLABS)
             pltpu.make_async_remote_copy(
@@ -318,20 +321,27 @@
             return carry
 
         lax.fori_loop(1, SLABS, one, 0, unroll=4)
-        own(stage, name, index).start()
-
-    def arrived(stage, name, index):
-        own(stage, name, index).wait()
+        own(stage, index).start()
+
+    def arrived(stage, index):
+        name = messages[stage][index]
+        own(stage, index).wait()
         bulk = recv.at[(stage,) + place(name, pl.ds(0, SLABS - 1))]
         pltpu.make_async_copy(bulk, bulk, recv_sem.at[stage, index]).wait()
 
-    def left(stage, name, index):
+    def left(stage, index):
+        name = messages[stage][index]
         bulk = send.at[(stage,) + place(name, pl.ds(0, SLABS - 1))]
         pltpu.make_async_copy(bulk, bulk, send_sem.at[stage, index]).wait()
 
     both = slice(None)
-    out_names = [(both, 0, 1), (both, 1, 1), (0, 2, 1), (0, 3, 1), (1, 2, 2)]
-    back_names = [(0, 0, 4), (1, 0, 1), (1, 1, 1), (1, 2, 1), (1, 3, 1)]
+    messages = []
+    for step in range(STEPS):
+        if step == 0:
+            messages.append([(0, 0, 4), (1, 0, 4)])
+        else:
+            messages.append([(both, 0, 1), (0, 1, 1), (0, 2, 1), (0, 3, 1), (1, 1, 3)])
+        messages.append([(0, 0, 4), (1, 0, 1), (1, 1, 1), (1, 2, 1), (1, 3, 1)])
 
     def across(step, rows):
         lines = pl.ds(rows * 8, 8)
@@ -344,39 +354,28 @@
             device_id_type=MESH,
         )
 
-    def send_rows(stage, group):
-        start(stage, out_names[group], group)
-        if group == 3:
-            start(stage, out_names[4], 4)
-
     need(*names[:4])
     for name in names[4:]:
         loads[name].start()
     for group in range(4):
         z_forward(t["velocity"], group, send.at[0], t)
-        if group == 0:
-            pl.semaphore_wait(barrier, SLABS)
-        send_rows(0, group)
+    pl.semaphore_wait(barrier, SLABS)
+    start(0, 0)
+    start(0, 1)
     need("kernel", "history")
     past_sums(t["kernel"], t["history"], sums)
     need(*tuple(loads))
     for step in range(STEPS):
         there, back = 2 * step, 2 * step + 1
         last = step == STEPS - 1
-        for index in range(4):
-            arrived(there, out_names[index], index)
-        spectrum_phase(step, 0, recv.at[there], t["kernel"], sums, send.at[back], t, middle, wide)
-        start(back, back_names[0], 0)
-        arrived(there, out_names[4], 4)
-        spectrum_phase(step, 1, recv.at[there], t["kernel"], sums, send.at[back], t, middle, wide)
-        for group in range(4):
-            start(back, back_names[1 + group], 1 + group)
-        arrived(back, back_names[0], 0)
-        for group in range(4):
-            arrived(back, back_names[1 + group], 1 + group)
+        final = len(messages[there]) - 1
+
+        def to_force(group):
+            arrived(back, 1 + group)
             z_inverse(recv.at[back], group, force.at[step], t)
             across(step, group).start()
-        for group in range(4):
+
+        def to_speed(group):
             across(step, group).wait_recv()
             friction(
                 group, side == 0, impedance, force.at[step], other.at[step], t["prestress"], t["strength"],
@@ -384,11 +383,33 @@
             )
             if not last:
                 z_forward(t["velocity"], group, send.at[2 * step + 2], t)
-                send_rows(2 * step + 2, group)
+                start(2 * step + 2, group)
+
+        for index in range(final):
+            arrived(there, index)
+        spectrum_phase(step, 0, recv.at[there], t["kernel"], sums, send.at[back], t, middle, wide)
+        start(back, 0)
+        arrived(there, final)
+        spectrum_phase(step, 1, recv.at[there], t["kernel"], sums, send.at[back], t, middle, wide)
+        for group in range(4):
+            start(back, 1 + group)
+        arrived(back, 0)
+        for group in range(3):
+            to_force(group)
+        if last:
+            to_force(3)
+            to_speed(0)
+        else:
+            to_speed(0)
+            to_force(3)
+        for group in range(1, 4):
+            to_speed(group)
+        if not last:
+            start(2 * step + 2, 4)
     state_out[...] = t["state"][...]
     for stage in range(2 * STEPS):
-        for index, name in enumerate(back_names if stage % 2 else out_names):
-            left(stage, name, index)
+        for index in range(len(messages[stage])):
+            left(stage, index)
     for step in range(STEPS):
         for group in range(4):
             across(step, group).wait_send()

time: 136 us -> 130 us (0.956)
  Pallas kernels: 135 us -> 129 us
    pallas_call x1, Pallas kernels: 133 us -> 126 us  [local(): pl.pallas_call(simulate, out_shape=(field, field, field), in_specs=[whole...]
where the time goes in v4:
time: 130 us
  Pallas kernels  129 us (99%)
    pallas_call x1, Pallas kernels, local(): pl.pallas_call(simulate, out_shape=(field, field, field), in_specs=[whole...  126 us

profile of v4, /device:TPU:1, one launch (start us, length us, event | category | flops | bytes accessed | tf_op | source)
XLA Modules:
  0.0 129.6 jit_solution(14838497405448972440)
XLA Ops:
  0.6 126.5 %simulate.1 = (f32[32,4096]{1,0:T(8,128)}, f32[32,4096]{1,0:T(8,128)}, f32[32,4096]{1,0:T(8,128)}) custom-call(f32[2]{0:T(128)} %refs_0_.1, f32[32,4096]{1,0:T(8,128)} %bitcast.6, bf16[512,768]{1,0:T(8,128)(2,1)} %constant.20.clone.refs_2_, bf16[256,768]{1,0:T(8,128)(2,1)} %constant.24.clone.refs_3_, f32[2,256,128]{2,1,0:T(8,128)} %constant.29.clone.refs_4_, ...), custom_call_target="tpu_custom_call" | custom-call | tf_op jit(solution)/shard_map/simulate/pallas_call | solution.py:437
  127.1 2.5 %hand_over.1 = (f32[32,4096]{1,0:T(8,128)}, f32[32,4096]{1,0:T(8,128)}, f32[32,4096]{1,0:T(8,128)}) custom-call(f32[32,4096]{1,0:T(8,128)} %get-tuple-element.9.refs_0_, f32[32,4096]{1,0:T(8,128)} %get-tuple-element.10.refs_1_, f32[32,4096]{1,0:T(8,128)} %get-tuple-element.11.refs_2_), custom_call_target="tpu_custom_call" | custom-call | tf_op jit(solution)/shard_map/hand_over/pallas_call | solution.py:463

commit v5 on v4

--- a/solution.py
+++ b/solution.py
@@ -341,7 +341,7 @@
             messages.append([(0, 0, 4), (1, 0, 4)])
         else:
             messages.append([(both, 0, 1), (0, 1, 1), (0, 2, 1), (0, 3, 1), (1, 1, 3)])
-        messages.append([(0, 0, 4), (1, 0, 1), (1, 1, 1), (1, 2, 1), (1, 3, 1)])
+        messages.append([(0, 0, 3), (1, 0, 1), (1, 1, 1), (1, 2, 1), (both, 3, 1)])
 
     def across(step, rows):
         lines = pl.ds(rows * 8, 8)

time: 130 us -> 127 us (0.977)
  Pallas kernels: 129 us -> 125 us
    pallas_call x1, Pallas kernels: 126 us -> 123 us  [local(): pl.pallas_call(simulate, out_shape=(field, field, field), in_specs=[whole...]
where the time goes in v5:
time: 127 us; the launch traced here: 126 us
  Pallas kernels  125 us (98%)
    pallas_call x1, Pallas kernels, local(): pl.pallas_call(simulate, out_shape=(field, field, field), in_specs=[whole...  123 us

profile of v5, /device:TPU:1, one launch (start us, length us, event | category | flops | bytes accessed | tf_op | source)
XLA Modules:
  0.0 126.0 jit_solution(18199891945717796720)
XLA Ops:
  0.6 122.8 %simulate.1 = (f32[32,4096]{1,0:T(8,128)}, f32[32,4096]{1,0:T(8,128)}, f32[32,4096]{1,0:T(8,128)}) custom-call(f32[2]{0:T(128)} %refs_0_.1, f32[32,4096]{1,0:T(8,128)} %bitcast.6, bf16[512,768]{1,0:T(8,128)(2,1)} %constant.20.clone.refs_2_, bf16[256,768]{1,0:T(8,128)(2,1)} %constant.24.clone.refs_3_, f32[2,256,128]{2,1,0:T(8,128)} %constant.29.clone.refs_4_, ...), custom_call_target="tpu_custom_call" | custom-call | tf_op jit(solution)/shard_map/simulate/pallas_call | solution.py:437
  123.5 2.5 %hand_over.1 = (f32[32,4096]{1,0:T(8,128)}, f32[32,4096]{1,0:T(8,128)}, f32[32,4096]{1,0:T(8,128)}) custom-call(f32[32,4096]{1,0:T(8,128)} %get-tuple-element.9.refs_0_, f32[32,4096]{1,0:T(8,128)} %get-tuple-element.10.refs_1_, f32[32,4096]{1,0:T(8,128)} %get-tuple-element.11.refs_2_), custom_call_target="tpu_custom_call" | custom-call | tf_op jit(solution)/shard_map/hand_over/pallas_call | solution.py:463
